TPU v7x, 32 devices: a whole 2x2x4 slice. The times are simulated.
32 devices in a mesh: parts: 2 (over x), scene: 4 (over y, core), range: 4 (over z).
Axes of the slice: x: 2, y: 2, z: 4, core: 2. Of those that a mesh axis runs over, the one named last changes fastest.
Arguments:
- secondary: bfloat16 [16, 1056, 2, 1024], P(('parts', 'scene'), None, None, 'range'), parts along dimension 0, may hold values from -6 to 6
- reference_store: bfloat16 [8, 4, 256, 2, 1024], P(('parts', 'scene'), None, None, None, 'range'), parts along dimension 0, may hold values from -6 to 6
- tile_owner: int32 [8], P('parts'), parts along dimension 0, may hold values from 0 to 3
- az_kernel: float32 [64, 8], replicated, may hold values from -2 to 2
- rg_kernel: float32 [64, 8], replicated, may hold values from -2 to 2
- az_offset: int32 [16, 1024], P(('parts', 'scene')), parts along dimension 0, may hold values from -12 to 12
- az_index: int32 [16, 1024], P(('parts', 'scene')), parts along dimension 0, may hold values from 0 to 63
- rg_offset: int32 [16, 1024], P(('parts', 'scene'), 'range'), parts along dimension 0, may hold values from -12 to 12
- rg_index: int32 [16, 1024], P(('parts', 'scene'), 'range'), parts along dimension 0, may hold values from 0 to 63
Outputs:
- reference_pairs: float32 [16, 2, 256, 64], P(('parts', 'scene'), None, None, 'range'), parts along dimension 0
- sequential_pairs: float32 [16, 2, 256, 64], P(('parts', 'scene'), None, None, 'range'), parts along dimension 0
- coherence: float32 [16, 256, 64], P(('parts', 'scene'), None, 'range'), parts along dimension 0
There are 2 independent parts, one for each index of `parts`. A program takes and returns all parts, laid end to end along the dimension named above; an argument that names none is the same for every part. Nothing has to cross between parts.
Inputs may be any that keep to these rules, and one draw needn't show every extreme that they name: `tile_owner`: the scene device holding reference tile s.
All inputs are finite; a program needn't handle non-finite values.
Results may differ from a plain program's by a relative error of at most 0.008.
Values may be sent and summed in bfloat16 or wider, within the bound.
A program may use at most 128 MiB of HBM per device.

v0:
```python
import functools

import jax
import jax.numpy as jnp
from jax import lax
from jax.experimental import pallas as pl
from jax.experimental.pallas import tpu as pltpu
from jax.sharding import PartitionSpec as P

LOOK_AZ = 4
LOOK_RG = 16
LANES = 128

eps_power = 1e-06
F32 = jnp.float32
BF16 = jnp.bfloat16
MESH = pl.DeviceIdType.MESH


def iota(shape, dim):
    return lax.broadcasted_iota(jnp.int32, shape, dim)


def flag(condition):
    return jnp.where(condition, 1.0, 0.0).astype(BF16)


def matmul(a, b, contract=((1,), (0,))):
    return lax.dot_general(a, b, (contract, ((), ())), preferred_element_type=F32)


def tap_table(kernel, stride):
    count, taps = kernel.shape
    place = flag(iota((taps, LANES), 1) == stride * iota((taps, LANES), 0))
    spread = matmul(kernel.astype(BF16), place).astype(BF16)
    ones = flag(iota((16, LANES), 0) == 0)
    return jnp.concatenate(
        [
            jnp.concatenate([spread, jnp.zeros((count, LANES), BF16)], 1),
            jnp.concatenate([jnp.zeros((16, LANES), BF16), ones], 1),
        ],
        0,
    )


def looked_up(table, index, offset):
    count = table.shape[0] - 16
    length = index.shape[1]
    one_hot = flag(iota((count, length), 0) == index)
    shift = jnp.broadcast_to(offset.astype(F32), (16, length)).astype(BF16)
    return matmul(jnp.concatenate([one_hot, shift], 0), table, ((0,), (0,)))


def banded(taps, place, reach):
    inside = (place >= 0) & (place < reach)
    picked = jnp.take_along_axis(taps, place & (LANES - 1), axis=1, mode="promise_in_bounds")
    return jnp.where(inside, picked, 0.0).astype(BF16)


def kernel_body(
    dims,
    sec_hbm, store_hbm, owner_ref, azk_ref, rgk_ref, azo_ref, azi_ref, rgo_ref, rgi_ref,
    pair_ref, seq_ref, coh_ref,
    sec, store, own, z, cur, az_mat, rg_mat, rg_halo, table, perm, edge, halo,
    recv_f, recv_b, send_f, send_b, ret_s, ret_r,
    sec_sem, store_sem, edge_sem, halo_sem, fs_sem, fr_sem, bs_sem, br_sem, rs_sem, rr_sem,
):
    scenes, tiles, rows, cols, margin, taps, n_scene, n_range = dims
    looks = rows // LOOK_AZ
    cells = cols // LOOK_RG
    wide = 2 * (rows + 2 * margin)
    both = 2 * rows
    me = lax.axis_index("scene")
    col = lax.axis_index("range")
    at_first, at_last = me == 0, me == n_scene - 1
    has_left, has_right = col > 0, col < n_range - 1
    sides = (
        (has_left, {"range": col - 1}),
        (has_right, {"range": col + 1}),
        (me > 0, {"scene": me - 1}),
        (me < n_scene - 1, {"scene": me + 1}),
    )

    def load_store(s):
        source = store_hbm.reshape(tiles, both, cols).at[s]
        return pltpu.make_async_copy(source, store.at[s], store_sem.at[s])

    def load_sec(k):
        length = sec.shape[1]
        source = sec_hbm.reshape(scenes, length, cols).at[k]
        return pltpu.make_async_copy(source, sec.at[k], sec_sem.at[k])

    for k in range(scenes):
        load_sec(k).start()
    for s in range(tiles):
        load_store(s).start()

    barrier = pltpu.get_barrier_semaphore()
    for exists, device in sides:
        @pl.when(exists)
        def _():
            pl.semaphore_signal(barrier, inc=1, device_id=device, device_id_type=MESH)

    @pl.when(jnp.logical_not(has_left))
    def _():
        halo[:, 0] = jnp.zeros(halo.shape[:1] + halo.shape[2:], BF16)

    @pl.when(jnp.logical_not(has_right))
    def _():
        halo[:, 1] = jnp.zeros(halo.shape[:1] + halo.shape[2:], BF16)

    @pl.when(at_first)
    def _():
        recv_f[...] = jnp.zeros_like(recv_f)
        ret_r[...] = jnp.zeros_like(ret_r)

    @pl.when(at_last)
    def _():
        recv_b[...] = jnp.zeros_like(recv_b)

    table[...] = tap_table(azk_ref[...], 2)
    order = iota((rows, rows), 0)
    perm[...] = flag(iota((rows, rows), 1) == LOOK_AZ * (order % looks) + order // looks)
    rg_table = tap_table(rgk_ref[...], 1)
    for k in range(scenes):
        found = looked_up(rg_table, rgi_ref[k : k + 1, :], rgo_ref[k : k + 1, :])
        tap_rows, shift = found[:, :LANES], found[:, LANES:].astype(jnp.int32)
        lane = iota((cols, LANES), 1)
        start = iota((cols, LANES), 0) + shift + (margin - 3)
        for t in range(cols // LANES):
            rg_mat[k, :, t * LANES : (t + 1) * LANES] = banded(
                tap_rows, lane + (t * LANES + margin) - start, taps
            )
        beside = jnp.where(lane < margin, lane, lane + cols)
        beside = jnp.where(lane < 2 * margin, beside, 4 * cols)
        outer = banded(tap_rows, beside - start, taps).astype(F32)
        rg_halo[k] = jnp.transpose(outer)[: 2 * margin].astype(BF16)

    def edge_copy(s, side):
        to = {"range": col - 1} if side == 0 else {"range": col + 1}
        return pltpu.make_async_remote_copy(
            src_ref=edge.at[s, side],
            dst_ref=halo.at[s, 1 - side],
            send_sem=edge_sem.at[s, side],
            recv_sem=halo_sem.at[s, 1 - side],
            device_id=to,
            device_id_type=MESH,
        )

    def halo_arrival(s, side):
        return edge_copy(s, 1 - side)

    def line_copy(s, forward):
        if forward:
            source, target, sent, got, to = send_f, recv_f, fs_sem, fr_sem, me + 1
        else:
            source, target, sent, got, to = send_b, recv_b, bs_sem, br_sem, me - 1
        return pltpu.make_async_remote_copy(
            src_ref=source.at[s],
            dst_ref=target.at[s],
            send_sem=sent.at[s],
            recv_sem=got.at[s],
            device_id={"scene": to},
            device_id_type=MESH,
        )

    def result_copy(s):
        return pltpu.make_async_remote_copy(
            src_ref=ret_s.at[s],
            dst_ref=ret_r.at[s],
            send_sem=rs_sem.at[s],
            recv_sem=rr_sem.at[s],
            device_id={"scene": me + 1},
            device_id_type=MESH,
        )

    def azimuth(s):
        for k in range(scenes):
            here = pl.ds(pl.multiple_of(s * rows, rows), rows)
            found = looked_up(table[...], azi_ref[k : k + 1, here], azo_ref[k : k + 1, here])
            found = matmul(perm[...], found.astype(BF16))
            for l in range(LOOK_AZ):
                part = found[l * looks : (l + 1) * looks]
                tap_rows, shift = part[:, :LANES], part[:, LANES:].astype(jnp.int32)
                row = LOOK_AZ * iota((looks, LANES), 0) + l
                start = iota((looks, LANES), 1) - 2 * (row + shift + (margin - 3))
                for p in range(2):
                    for t in range(az_mat.shape[1] // LANES):
                        top = p * rows + l * looks
                        az_mat[top : top + looks, t * LANES : (t + 1) * LANES] = banded(
                            tap_rows, start + (t * LANES - p), 2 * taps
                        )
            lines = sec[k, pl.ds(pl.multiple_of(s * both, both), wide), :]
            z[s, k] = matmul(az_mat[:, :wide], lines).astype(BF16)
            which = iota((2 * margin, cols), 0)
            which = jnp.where(which < margin, which, which + cols - 2 * margin)
            ends = matmul(flag(iota((2 * margin, cols), 1) == which), z[s, k], ((1,), (1,)))
            ends = ends.astype(BF16)
            edge[s, 0, k] = ends[:margin]
            edge[s, 1, k] = ends[margin:]

        @pl.when(has_left)
        def _():
            edge_copy(s, 0).start()

        @pl.when(has_right)
        def _():
            edge_copy(s, 1).start()

    def range_step(s):
        @pl.when(has_left)
        def _():
            halo_arrival(s, 0).wait_recv()

        @pl.when(has_right)
        def _():
            halo_arrival(s, 1).wait_recv()

        for k in range(scenes):
            beside = jnp.concatenate([halo[s, 0, k], halo[s, 1, k]], 0)
            total = matmul(z[s, k], rg_mat[k], ((1,), (1,)))
            total = total + matmul(beside, rg_halo[k], ((0,), (0,)))
            cur[s, k] = total.astype(BF16)

    def pass_on(s, forward, from_here):
        owner = owner_ref[s]
        if forward:
            instead = cur[s, scenes - 1]
            if not from_here:
                line_copy(s, True).wait_recv()
                instead = jnp.where(owner < me, recv_f[s], instead)
            send_f[s] = jnp.where(owner == me, own[s], instead)
        else:
            instead = cur[s, 0]
            if not from_here:
                line_copy(s, False).wait_recv()
                instead = jnp.where(owner > me, recv_b[s], instead)
            send_b[s] = jnp.where(owner == me, own[s], instead)
        line_copy(s, forward).start()

    inner = jnp.logical_not(at_first) & jnp.logical_not(at_last)
    early_f = inner & (me == 1)
    early_b = inner & (me == n_scene - 2) & jnp.logical_not(early_f)

    def early(s):
        @pl.when(early_f)
        def _():
            pass_on(s, True, False)

        @pl.when(early_b)
        def _():
            pass_on(s, False, False)

    for k in range(scenes):
        load_sec(k).wait()
    pl.semaphore_wait(barrier, sum(exists.astype(jnp.int32) for exists, _ in sides))
    azimuth(0)
    for s in range(tiles):
        load_store(s).wait()
    line = iota((both, both), 0)
    pick = 2 * (LOOK_AZ * (line % looks) + (line % rows) // looks) + line // rows
    pick = flag(iota((both, both), 1) == pick)
    for s in range(tiles):
        own[s] = matmul(pick, store[s]).astype(BF16)

    def resample(s, carry):
        @pl.when(s + 1 < tiles)
        def _():
            azimuth(s + 1)

        range_step(s)

        @pl.when(at_first)
        def _():
            pass_on(s, True, True)

        @pl.when(at_last)
        def _():
            pass_on(s, False, True)

        @pl.when(s > 0)
        def _():
            early(s - 1)

        return carry

    lax.fori_loop(0, tiles, resample, 0)
    early(tiles - 1)

    mean = flag(iota((cols, cells), 0) // LOOK_RG == iota((cols, cells), 1))

    def row_sums(*makers):
        sums = None
        for l in range(LOOK_AZ):
            terms = makers[0](l)
            sums = terms if sums is None else [a + b for a, b in zip(sums, terms)]
        return sums

    def multilooked(sums):
        stacked = jnp.concatenate(sums, 0)
        high = stacked.astype(BF16)
        low = (stacked - high.astype(F32)).astype(BF16)
        found = (matmul(high, mean) + matmul(low, mean)) * (1.0 / (LOOK_AZ * LOOK_RG))
        return [found[i * looks : (i + 1) * looks] for i in range(len(sums))]

    def cross(a, b):
        return [a[0] * b[0] + a[1] * b[1], a[1] * b[0] - a[0] * b[1]]

    def power(a):
        return a[0] * a[0] + a[1] * a[1]

    def coherence(re, im, first, second):
        return jnp.sqrt(re * re + im * im) / jnp.sqrt(first * second + eps_power)

    def compare(s, carry):
        @pl.when(inner & jnp.logical_not(early_f))
        def _():
            pass_on(s, True, False)

        @pl.when(inner & jnp.logical_not(early_b))
        def _():
            pass_on(s, False, False)

        @pl.when(at_first)
        def _():
            line_copy(s, False).wait_recv()

        @pl.when(at_last)
        def _():
            line_copy(s, True).wait_recv()

        owner = owner_ref[s]

        def terms(l):
            def parts(read):
                return [
                    read(slice(p * rows + l * looks, p * rows + (l + 1) * looks)).astype(F32)
                    for p in range(2)
                ]

            images = [parts(lambda at, k=k: cur[s, k, at, :]) for k in range(scenes)]
            before = parts(lambda at: recv_f[s, at, :])
            after = parts(lambda at: recv_b[s, at, :])
            mine = parts(lambda at: own[s, at, :])
            ref = [
                jnp.where(owner == me, o, jnp.where(owner < me, f, b))
                for o, f, b in zip(mine, before, after)
            ]
            before = [jnp.where(at_first, r, f) for r, f in zip(ref, before)]
            chain = [before] + images + [after]
            out = []
            for image in images:
                out += cross(ref, image)
            for one, two in zip(chain[:-1], chain[1:]):
                out += cross(one, two)
            return out + [power(image) for image in chain]

        found = multilooked(row_sums(terms))
        pairs = found[: 2 * scenes]
        seqs = found[2 * scenes : 4 * scenes + 2]
        powers = found[4 * scenes + 2 :]
        at = pl.ds(pl.multiple_of(s * looks, looks), looks)
        for k in range(scenes + 1):
            re, im = seqs[2 * k], seqs[2 * k + 1]
            coherent = coherence(re, im, powers[k], powers[k + 1])
            if k < scenes:
                pair_ref[k, 0, at, :] = pairs[2 * k]
                pair_ref[k, 1, at, :] = pairs[2 * k + 1]
                seq_ref[k, 0, at, :] = re
                seq_ref[k, 1, at, :] = im
                coh_ref[k, at, :] = coherent
            else:
                for i, value in enumerate((re, im, coherent)):
                    ret_s[s, i] = value

        @pl.when(jnp.logical_not(at_last))
        def _():
            result_copy(s).start()

        return carry

    lax.fori_loop(0, tiles, compare, 0)

    def settle(s, carry):
        @pl.when(jnp.logical_not(at_first))
        def _():
            result_copy(s).wait_recv()
            returned = owner_ref[s] < me
            at = pl.ds(pl.multiple_of(s * looks, looks), looks)
            for p in range(2):
                seq_ref[0, p, at, :] = jnp.where(returned, ret_r[s, p], seq_ref[0, p, at, :])
            coh_ref[0, at, :] = jnp.where(returned, ret_r[s, 2], coh_ref[0, at, :])
            line_copy(s, False).wait_send()

        @pl.when(jnp.logical_not(at_last))
        def _():
            line_copy(s, True).wait_send()
            result_copy(s).wait_send()

        @pl.when(has_left)
        def _():
            edge_copy(s, 0).wait_send()

        @pl.when(has_right)
        def _():
            edge_copy(s, 1).wait_send()

        return carry

    lax.fori_loop(0, tiles, settle, 0)


def local(n_scene, n_range, *operands):
    secondary, store, _, az_kernel = operands[:4]
    scenes, length, parts, cols = secondary.shape
    _, tiles, rows = store.shape[:3]
    taps = az_kernel.shape[1]
    margin = (length - tiles * rows) // 2
    looks, cells = rows // LOOK_AZ, cols // LOOK_RG
    both = 2 * rows
    wide = -(-2 * (rows + 2 * margin) // LANES) * LANES
    image = (both, cols)
    dma = pltpu.SemaphoreType.DMA
    vmem = pl.BlockSpec(memory_space=pltpu.VMEM)
    hbm = pl.BlockSpec(memory_space=pl.ANY)
    smem = pl.BlockSpec(memory_space=pltpu.SMEM)
    strip = tiles * looks
    return pl.pallas_call(
        functools.partial(kernel_body, (scenes, tiles, rows, cols, margin, taps, n_scene, n_range)),
        out_shape=(
            jax.ShapeDtypeStruct((scenes, 2, strip, cells), F32),
            jax.ShapeDtypeStruct((scenes, 2, strip, cells), F32),
            jax.ShapeDtypeStruct((scenes, strip, cells), F32),
        ),
        in_specs=[hbm, hbm, smem] + [vmem] * 6,
        out_specs=(vmem, vmem, vmem),
        scratch_shapes=[
            pltpu.VMEM((scenes, 2 * length, cols), BF16),
            pltpu.VMEM((tiles,) + image, BF16),
            pltpu.VMEM((tiles,) + image, BF16),
            pltpu.VMEM((tiles, scenes) + image, BF16),
            pltpu.VMEM((tiles, scenes) + image, BF16),
            pltpu.VMEM((both, wide), BF16),
            pltpu.VMEM((scenes, cols, cols), BF16),
            pltpu.VMEM((scenes, 2 * margin, cols), BF16),
            pltpu.VMEM((az_kernel.shape[0] + 16, 2 * LANES), BF16),
            pltpu.VMEM((rows, rows), BF16),
            pltpu.VMEM((tiles, 2, scenes, margin, both), BF16),
            pltpu.VMEM((tiles, 2, scenes, margin, both), BF16),
            pltpu.VMEM((tiles,) + image, BF16),
            pltpu.VMEM((tiles,) + image, BF16),
            pltpu.VMEM((tiles,) + image, BF16),
            pltpu.VMEM((tiles,) + image, BF16),
            pltpu.VMEM((tiles, 3, looks, cells), F32),
            pltpu.VMEM((tiles, 3, looks, cells), F32),
            dma((scenes,)),
            dma((tiles,)),
            dma((tiles, 2)),
            dma((tiles, 2)),
            dma((tiles,)),
            dma((tiles,)),
            dma((tiles,)),
            dma((tiles,)),
            dma((tiles,)),
            dma((tiles,)),
        ],
        compiler_params=pltpu.CompilerParams(
            collective_id=0, has_side_effects=True, vmem_limit_bytes=48 << 20
        ),
    )(*operands)


def solution(mesh):
    in_specs = (
        P(("parts", "scene"), None, None, "range"),
        P(("parts", "scene"), None, None, None, "range"),
        P("parts"),
        P(),
        P(),
        P(("parts", "scene"), None),
        P(("parts", "scene"), None),
        P(("parts", "scene"), "range"),
        P(("parts", "scene"), "range"),
    )
    out_specs = (
        P(("parts", "scene"), None, None, "range"),
        P(("parts", "scene"), None, None, "range"),
        P(("parts", "scene"), None, "range"),
    )
    body = functools.partial(local, mesh.shape["scene"], mesh.shape["range"])
    return jax.shard_map(body, mesh=mesh, in_specs=in_specs, out_specs=out_specs, check_vma=False)
```

profile of v0, /device:TPU:0, one launch (start us, length us, event | category | flops | bytes accessed | tf_op | source)
XLA Modules:
  0.0 47.0 jit_solution(9699179593651803196)
XLA Ops:
  0.6 0.8 %copy.12.azk_ref = f32[64,8]{1,0:T(8,128)S(1)} copy(f32[64,8]{0,1:T(8,128)} %param.12) | data formatting | bytes 4096 | tf_op args[3]
  1.4 0.8 %copy.13.rgk_ref = f32[64,8]{1,0:T(8,128)S(1)} copy(f32[64,8]{0,1:T(8,128)} %param.13) | data formatting | bytes 4096 | tf_op args[4]
  2.2 0.0 copy-start
  2.2 1.6 %copy-done = bf16[2,1056,2,256]{3,2,1,0:T(2,128)(2,1)S(1)} copy-done((bf16[2,1056,2,256]{3,2,1,0:T(2,128)(2,1)S(1)}, bf16[2,1056,2,256]{3,2,1,0:T(2,128)(2,1)}, u32[]{:S(2)}) %copy-start) | copy-done | bytes 2162712
  3.8 0.0 copy-start.1
  3.8 1.2 %copy-done.1 = bf16[1,4,256,2,256]{4,3,2,1,0:T(2,128)(2,1)S(1)} copy-done((bf16[1,4,256,2,256]{4,3,2,1,0:T(2,128)(2,1)S(1)}, bf16[1,4,256,2,256]{4,3,2,1,0:T(2,128)(2,1)}, u32[]{:S(2)}) %copy-start.1) | copy-done | bytes 1048600
  5.0 0.0 copy-start.2
  5.0 0.7 %copy-done.2 = s32[2,1024]{1,0:T(2,128)S(1)} copy-done((s32[2,1024]{1,0:T(2,128)S(1)}, s32[2,1024]{1,0:T(2,128)}, u32[]{:S(2)}) %copy-start.2) | copy-done | bytes 8216
  5.7 0.0 copy-start.3
  5.7 0.7 %copy-done.3 = s32[2,1024]{1,0:T(2,128)S(1)} copy-done((s32[2,1024]{1,0:T(2,128)S(1)}, s32[2,1024]{1,0:T(2,128)}, u32[]{:S(2)}) %copy-start.3) | copy-done | bytes 8216
  6.4 0.0 copy-start.4
  6.4 0.7 %copy-done.4 = s32[2,256]{1,0:T(2,128)S(1)} copy-done((s32[2,256]{1,0:T(2,128)S(1)}, s32[2,256]{1,0:T(2,128)}, u32[]{:S(2)}) %copy-start.4) | copy-done | bytes 2072
  7.1 0.0 copy-start.5
  7.1 0.7 %copy-done.5 = s32[2,256]{1,0:T(2,128)S(1)} copy-done((s32[2,256]{1,0:T(2,128)S(1)}, s32[2,256]{1,0:T(2,128)}, u32[]{:S(2)}) %copy-start.5) | copy-done | bytes 2072
  7.8 0.0 copy-start.6
  7.8 0.7 %copy-done.6 = s32[4]{0:T(128)S(1)} copy-done((s32[4]{0:T(128)S(1)}, s32[4]{0:T(128)}, u32[]{:S(2)}) %copy-start.6) | copy-done | bytes 40
  8.4 36.3 %shard_map.112 = (f32[2,2,256,16]{3,2,1,0:T(8,128)S(1)}, f32[2,2,256,16]{3,2,1,0:T(8,128)S(1)}, f32[2,256,16]{2,1,0:T(8,128)S(1)}) custom-call(bf16[2,1056,2,256]{3,2,1,0:T(2,128)(2,1)S(1)} %copy-done, bf16[1,4,256,2,256]{4,3,2,1,0:T(2,128)(2,1)S(1)} %copy-done.1, s32[4]{0:T(128)S(1)} %copy-done.6, f32[64,8]{1,0:T(8,128)S(1)} %copy.12.azk_ref, ...), custom_call_target="tpu_custom_call" | custom-call | tf_op jit(solution)/shard_map/pallas_call | solution.py:428
  44.7 0.8 %copy.14 = f32[2,2,256,16]{2,3,1,0:T(8,128)} copy(f32[2,2,256,16]{3,2,1,0:T(8,128)S(1)} %get-tuple-element.3) | data formatting | bytes 131072 | tf_op jit(solution)/shard_map/pallas_call | solution.py:428
  45.5 0.7 %copy.16 = f32[2,256,16]{1,2,0:T(8,128)} copy(f32[2,256,16]{2,1,0:T(8,128)S(1)} %get-tuple-element.5) | data formatting | bytes 65536 | tf_op jit(solution)/shard_map/pallas_call | solution.py:428
  46.2 0.8 %copy.15 = f32[2,2,256,16]{2,3,1,0:T(8,128)} copy(f32[2,2,256,16]{3,2,1,0:T(8,128)S(1)} %get-tuple-element.4) | data formatting | bytes 131072 | tf_op jit(solution)/shard_map/pallas_call | solution.py:428
Async XLA Ops:
  2.2 1.6 %copy-start = (bf16[2,1056,2,256]{3,2,1,0:T(2,128)(2,1)S(1)}, bf16[2,1056,2,256]{3,2,1,0:T(2,128)(2,1)}, u32[]{:S(2)}) copy-start(bf16[2,1056,2,256]{3,2,1,0:T(2,128)(2,1)} %sec_hbm.1) | copy-start | bytes 6488068
  3.8 1.2 %copy-start.1 = (bf16[1,4,256,2,256]{4,3,2,1,0:T(2,128)(2,1)S(1)}, bf16[1,4,256,2,256]{4,3,2,1,0:T(2,128)(2,1)}, u32[]{:S(2)}) copy-start(bf16[1,4,256,2,256]{4,3,2,1,0:T(2,128)(2,1)} %store_hbm.1) | copy-start | bytes 3145732
  5.0 0.7 %copy-start.2 = (s32[2,1024]{1,0:T(2,128)S(1)}, s32[2,1024]{1,0:T(2,128)}, u32[]{:S(2)}) copy-start(s32[2,1024]{1,0:T(2,128)} %azo_ref.1) | copy-start | bytes 24580
  5.7 0.7 %copy-start.3 = (s32[2,1024]{1,0:T(2,128)S(1)}, s32[2,1024]{1,0:T(2,128)}, u32[]{:S(2)}) copy-start(s32[2,1024]{1,0:T(2,128)} %azi_ref.1) | copy-start | bytes 24580
  6.4 0.7 %copy-start.4 = (s32[2,256]{1,0:T(2,128)S(1)}, s32[2,256]{1,0:T(2,128)}, u32[]{:S(2)}) copy-start(s32[2,256]{1,0:T(2,128)} %rgo_ref.1) | copy-start | bytes 6148
  7.1 0.7 %copy-start.5 = (s32[2,256]{1,0:T(2,128)S(1)}, s32[2,256]{1,0:T(2,128)}, u32[]{:S(2)}) copy-start(s32[2,256]{1,0:T(2,128)} %rgi_ref.1) | copy-start | bytes 6148
  7.8 0.7 %copy-start.6 = (s32[4]{0:T(128)S(1)}, s32[4]{0:T(128)}, u32[]{:S(2)}) copy-start(s32[4]{0:T(128)} %owner_ref.1) | copy-start | bytes 52
where the time goes:
time: 47.5 us; the launch traced here: 47 us
  Pallas kernels  36.3 us (76%)
  local copies, waits for them, and re-layouts  10.1 us (21%)
  between operations  0.65 us (1%)
    pallas_call x1, Pallas kernels, local(): pl.pallas_call(functools.partial(kernel_body, (scenes, tiles, rows, cols,...  36.3 us
    unnamed x16, local copies, waits for them, and re-layouts  7.78 us
    pallas_call x3, local copies, waits for them, and re-layouts, local(): pl.pallas_call(functools.partial(kernel_body, (scenes, tiles, rows, cols,...  2.32 us

commit v1 on v0

v1 whole, which is shorter than its diff:
```python
import functools

import jax
import jax.numpy as jnp
from jax import lax
from jax.experimental import pallas as pl
from jax.experimental.pallas import tpu as pltpu
from jax.sharding import PartitionSpec as P

LOOK_AZ = 4
LOOK_RG = 16
LANES = 128
GROUP = 16
VMEM_BYTES = 62 << 20

eps_power = 1e-06
F32 = jnp.float32
BF16 = jnp.bfloat16
MESH = pl.DeviceIdType.MESH


def iota(shape, dim):
    return lax.broadcasted_iota(jnp.int32, shape, dim)


def flag(condition):
    return jnp.where(condition, 1.0, 0.0).astype(BF16)


def matmul(a, b, contract=((1,), (0,))):
    return lax.dot_general(a, b, (contract, ((), ())), preferred_element_type=F32)


def tap_table(kernel, stride):
    taps, count = kernel.shape
    place = flag(iota((taps, LANES), 1) == stride * iota((taps, LANES), 0))
    spread = matmul(kernel.astype(BF16), place, ((0,), (0,))).astype(BF16)
    ones = flag(iota((GROUP, LANES), 0) == 0)
    return jnp.concatenate(
        [
            jnp.concatenate([spread, jnp.zeros((count, LANES), BF16)], 1),
            jnp.concatenate([jnp.zeros((GROUP, LANES), BF16), ones], 1),
        ],
        0,
    )


def looked_up(table, index, offset):
    count = table.shape[0] - GROUP
    length = index.shape[1]
    one_hot = flag(iota((count, length), 0) == index)
    shift = jnp.broadcast_to(offset.astype(F32), (GROUP, length)).astype(BF16)
    return matmul(jnp.concatenate([one_hot, shift], 0), table, ((0,), (0,)))


def banded(taps, place, reach):
    if reach & (reach - 1):
        inside = (place >= 0) & (place < reach)
    else:
        inside = (place & -reach) == 0
    picked = jnp.take_along_axis(taps, place & (LANES - 1), axis=1, mode="promise_in_bounds")
    return jnp.where(inside, picked, 0.0).astype(BF16)


def cross(a, b):
    return [a[0] * b[0] + a[1] * b[1], a[1] * b[0] - a[0] * b[1]]


def power(a):
    return a[0] * a[0] + a[1] * a[1]


def coherence(re, im, first, second):
    return jnp.sqrt(re * re + im * im) / jnp.sqrt(first * second + eps_power)


def kernel_body(
    dims,
    sec_hbm, store_hbm, owner_hbm, azk_hbm, rgk_hbm, azo_hbm, azi_hbm, rgo_hbm, rgi_hbm,
    pair_ref, seq_ref, coh_ref,
    owner_ref, azk, rgk, azo, azi, rgo, rgi,
    sec, store, other, own, z, cur, az_mat, rg_mat, rg_halo, table, edge, halo,
    comm, relayed, y_send, ref, stats, packed, ret_s, ret_r,
    small_sem, sec_sem, store_sem, edge_sem, halo_sem, xs_sem, xr_sem, hs_sem, hr_sem,
    ys_sem, yr_sem, ls_sem, lr_sem, rs_sem, rr_sem,
):
    scenes, tiles, rows, cols, margin, taps, n_scene, n_range = dims
    looks = rows // LOOK_AZ
    both = 2 * rows
    deep = LOOK_AZ * GROUP
    blocks = rows // deep
    lines = 2 * (tiles * rows + 2 * margin)
    me = lax.axis_index("scene")
    col = lax.axis_index("range")
    core, chip = lax.rem(me, 2), lax.div(me, 2)
    is_l, is_r = core == 0, core == 1
    sibling = me + 1 - 2 * core
    outer = me - 1 + 2 * core
    has_prev, has_next = chip > 0, chip < n_scene // 2 - 1
    inner = has_prev & has_next
    l_up, r_up = is_l & has_prev, is_r & has_next
    has_outer = l_up | r_up
    has_left, has_right = col > 0, col < n_range - 1
    always = me >= 0
    sides = (
        (has_left, {"range": col - 1}),
        (has_right, {"range": col + 1}),
        (always, {"scene": sibling}),
        (has_outer, {"scene": outer}),
    )

    smalls = [
        pltpu.make_async_copy(source, target, small_sem.at[i])
        for i, (source, target) in enumerate(
            (
                (rgk_hbm, rgk), (rgo_hbm, rgo), (rgi_hbm, rgi), (azk_hbm, azk),
                (azo_hbm, azo), (azi_hbm, azi), (owner_hbm, owner_ref),
            )
        )
    ]

    def load_store(s):
        source = store_hbm.reshape(tiles, both, cols).at[s]
        return pltpu.make_async_copy(source, store.at[s], store_sem.at[s])

    def load_sec(k):
        source = sec_hbm.reshape(scenes, lines, cols).at[k]
        return pltpu.make_async_copy(source, sec.at[k, pl.ds(0, lines)], sec_sem.at[k])

    for copy in smalls:
        copy.start()
    for k in range(scenes):
        load_sec(k).start()
    for s in range(tiles):
        load_store(s).start()

    barrier = pltpu.get_barrier_semaphore()
    for exists, device in sides:
        @pl.when(exists)
        def _():
            pl.semaphore_signal(barrier, inc=1, device_id=device, device_id_type=MESH)

    @pl.when(jnp.logical_not(has_left))
    def _():
        halo[:, 0] = jnp.zeros(halo.shape[:1] + halo.shape[2:], BF16)

    @pl.when(jnp.logical_not(has_right))
    def _():
        halo[:, 1] = jnp.zeros(halo.shape[:1] + halo.shape[2:], BF16)

    def remote(source, target, sent, got, device):
        return pltpu.make_async_remote_copy(
            src_ref=source,
            dst_ref=target,
            send_sem=sent,
            recv_sem=got,
            device_id=device,
            device_id_type=MESH,
        )

    def edge_copy(s, side):
        return remote(
            edge.at[s, side],
            halo.at[s, 1 - side],
            edge_sem.at[s, side],
            halo_sem.at[s, 1 - side],
            {"range": col - 1 if side == 0 else col + 1},
        )

    def candidate_copy(s):
        return remote(store.at[s], other.at[s], xs_sem.at[s], xr_sem.at[s], {"scene": sibling})

    def handoff_copy(s):
        source = cur.at[s, scenes - 1]
        return remote(source, comm.at[0, s], hs_sem.at[s], hr_sem.at[s], {"scene": sibling})

    def line_copy(s):
        target = comm.at[1 - core, s]
        return remote(y_send.at[s], target, ys_sem.at[s], yr_sem.at[s], {"scene": outer})

    def relay_copy(s):
        source = comm.at[core, s]
        return remote(source, relayed.at[s], ls_sem.at[s], lr_sem.at[s], {"scene": sibling})

    def result_copy(s):
        return remote(ret_s.at[s], ret_r.at[s], rs_sem.at[s], rr_sem.at[s], {"scene": outer})

    for k in range(scenes):
        sec[k, lines:, :] = jnp.zeros((sec.shape[1] - lines, cols), BF16)

    for copy in smalls[:3]:
        copy.wait()
    rg_table = tap_table(rgk[...], 1)
    for k in range(scenes):
        found = looked_up(rg_table, rgi[k : k + 1, :], rgo[k : k + 1, :])
        tap_rows, shift = found[:, :LANES], found[:, LANES:].astype(jnp.int32)
        lane = iota((cols, LANES), 1)
        start = iota((cols, LANES), 0) + shift + (margin - 3)
        for t in range(cols // LANES):
            rg_mat[k, :, t * LANES : (t + 1) * LANES] = banded(
                tap_rows, lane + (t * LANES + margin) - start, taps
            )
        beside = jnp.where(lane < margin, lane, lane + cols)
        beside = jnp.where(lane < 2 * margin, beside, 4 * cols)
        outside = banded(tap_rows, beside - start, taps).astype(F32)
        rg_halo[k] = jnp.transpose(outside)[: 2 * margin].astype(BF16)
    for copy in smalls[3:]:
        copy.wait()
    table[...] = tap_table(azk[...], 2)

    def by_look(parts):
        shape = (parts, LOOK_AZ, GROUP, parts * deep)
        source = parts * (LOOK_AZ * iota(shape, 2) + iota(shape, 1)) + iota(shape, 0)
        return flag(iota(shape, 3) == source).reshape(parts * deep, parts * deep)

    def azimuth(s):
        order = by_look(1)
        for k in range(scenes):
            here = pl.ds(pl.multiple_of(s * rows, rows), rows)
            found = looked_up(table[...], azi[k : k + 1, here], azo[k : k + 1, here]).astype(BF16)
            for j in range(blocks):
                part = matmul(order, found[j * deep : (j + 1) * deep])
                tap_rows, shift = part[:, :LANES], part[:, LANES:].astype(jnp.int32)
                shape = (LOOK_AZ, GROUP, LANES)
                row = (LOOK_AZ * iota(shape, 1) + iota(shape, 0)).reshape(deep, LANES)
                start = iota((deep, LANES), 1) - 2 * (row + shift + (margin - 3))
                for p in range(2):
                    for t in range(2):
                        az_mat[
                            k, j, p * deep : (p + 1) * deep, t * LANES : (t + 1) * LANES
                        ] = banded(tap_rows, start + (t * LANES - p), 2 * taps)
            for j in range(blocks):
                first = pl.multiple_of(s * both + j * 2 * deep, 2 * deep)
                found = matmul(az_mat[k, j], sec[k, pl.ds(first, 2 * LANES), :])
                z[s, k, j * 2 * deep : (j + 1) * 2 * deep, :] = found.astype(BF16)
            which = iota((2 * margin, cols), 0)
            which = jnp.where(which < margin, which, which + cols - 2 * margin)
            ends = matmul(flag(iota((2 * margin, cols), 1) == which), z[s, k], ((1,), (1,)))
            ends = ends.astype(BF16)
            edge[s, 0, k] = ends[:margin]
            edge[s, 1, k] = ends[margin:]

        @pl.when(has_left)
        def _():
            edge_copy(s, 0).start()

        @pl.when(has_right)
        def _():
            edge_copy(s, 1).start()

    def range_step(s):
        @pl.when(has_left)
        def _():
            edge_copy(s, 1).wait_recv()

        @pl.when(has_right)
        def _():
            edge_copy(s, 0).wait_recv()

        for k in range(scenes):
            beside = jnp.concatenate([halo[s, 0, k], halo[s, 1, k]], 0)
            total = matmul(z[s, k], rg_mat[k], ((1,), (1,)))
            total = total + matmul(beside, rg_halo[k], ((0,), (0,)))
            cur[s, k] = total.astype(BF16)

    def line_send(s, from_relay):
        owner_chip = lax.div(owner_ref[s], 2)
        value = cur[s, core * (scenes - 1)]
        if from_relay:
            beyond = (is_r & (owner_chip < chip)) | (is_l & (owner_chip > chip))
            value = jnp.where(beyond, relayed[s], value)
        y_send[s] = jnp.where(owner_chip == chip, own[s], value)
        line_copy(s).start()

    pl.semaphore_wait(barrier, sum(exists.astype(jnp.int32) for exists, _ in sides))
    for s in range(tiles):
        load_store(s).wait()
        candidate_copy(s).start()
    for k in range(scenes):
        load_sec(k).wait()
    azimuth(0)

    def resample(s, carry):
        @pl.when(s + 1 < tiles)
        def _():
            azimuth(s + 1)

        range_step(s)

        @pl.when(is_l)
        def _():
            handoff_copy(s).start()

        candidate_copy(s).wait_recv()
        order = by_look(2)
        for j in range(blocks):
            at = slice(j * 2 * deep, (j + 1) * 2 * deep)
            chosen = jnp.where(owner_ref[s] == sibling, other[s, at, :], store[s, at, :])
            own[s, at, :] = matmul(order, chosen).astype(BF16)

        @pl.when(has_outer & jnp.logical_not(inner))
        def _():
            line_send(s, False)

        return carry

    lax.fori_loop(0, tiles, resample, 0)

    lane = iota((cols, LANES), 1) & (GROUP - 1)
    start = LOOK_RG * lane
    place = iota((cols, LANES), 0)
    mean = flag((place >= start) & (place < start + LOOK_RG))
    lane_group = iota((looks, LANES), 1)

    def multilooked(count, terms):
        sums = [[] for _ in range(count)]
        for j in range(blocks):
            total = None
            for l in range(LOOK_AZ):
                new = terms(j, l)
                total = new if total is None else [a + b for a, b in zip(total, new)]
            for one, value in zip(sums, total):
                one.append(value)
        stacked = jnp.concatenate([value for one in sums for value in one], 0)
        high = stacked.astype(BF16)
        low = (stacked - high.astype(F32)).astype(BF16)
        found = (matmul(high, mean) + matmul(low, mean)) * (1.0 / (LOOK_AZ * LOOK_RG))
        return [found[i * looks : (i + 1) * looks] for i in range(count)]

    def parts(read, j, l):
        first = j * 2 * deep + l * GROUP
        return [read(slice(first + p * deep, first + p * deep + GROUP)).astype(F32) for p in range(2)]

    def pack(values):
        out = values[-1]
        for i in range(len(values) - 2, -1, -1):
            out = jnp.where(lane_group < (i + 1) * GROUP, values[i], out)
        return out

    def own_terms(s, carry):
        def terms(j, l):
            images = [parts(lambda at, k=k: cur[s, k, at, :], j, l) for k in range(scenes)]
            out = [power(image) for image in images]
            for one, two in zip(images[:-1], images[1:]):
                out += cross(one, two)
            return out

        found = multilooked(scenes + 2 * (scenes - 1), terms)
        for i, value in enumerate(found):
            stats[s, i] = value
        return carry

    lax.fori_loop(0, tiles, own_terms, 0)

    def compare(s, carry):
        def arrived():
            line_copy(s).wait_recv()
            relay_copy(s).start()

        def handed():
            relay_copy(s).wait_recv()

            @pl.when(inner)
            def _():
                line_send(s, True)

        pl.when(l_up)(arrived)
        pl.when(is_r & has_prev)(handed)
        pl.when(r_up)(arrived)
        pl.when(is_l & has_next)(handed)

        @pl.when(is_r)
        def _():
            handoff_copy(s).wait_recv()

        @pl.when(r_up)
        def _():
            def terms(j, l):
                last = parts(lambda at: cur[s, scenes - 1, at, :], j, l)
                after = parts(lambda at: comm[1, s, at, :], j, l)
                return cross(last, after) + [power(after)]

            re, im, strength = multilooked(3, terms)
            coherent = coherence(re, im, stats[s, scenes - 1], strength)
            ret_s[s] = pack([re, im, re, im, coherent])
            result_copy(s).start()

        owner_chip = lax.div(owner_ref[s], 2)
        direct = (is_l & (owner_chip < chip)) | (is_r & (owner_chip > chip))
        far = jnp.where(direct, comm[core, s], relayed[s])
        ref[...] = jnp.where(owner_chip == chip, own[s], far)

        @pl.when(me == 0)
        def _():
            comm[0, s] = ref[...]

        def terms(j, l):
            images = [parts(lambda at, k=k: cur[s, k, at, :], j, l) for k in range(scenes)]
            given = parts(lambda at: ref[at, :], j, l)
            before = parts(lambda at: comm[0, s, at, :], j, l)
            out = cross(before, images[0]) + [power(before)]
            for image in images:
                out += cross(given, image)
            return out

        found = multilooked(3 + 2 * scenes, terms)
        strength = found[2]
        for k in range(scenes):
            if k == 0:
                re, im = found[0], found[1]
            else:
                re, im = stats[s, scenes + 2 * (k - 1)], stats[s, scenes + 2 * (k - 1) + 1]
            coherent = coherence(re, im, strength, stats[s, k])
            strength = stats[s, k]
            packed[k, s] = pack([found[3 + 2 * k], found[4 + 2 * k], re, im, coherent])
        return carry

    lax.fori_loop(0, tiles, compare, 0)

    def settle(s, carry):
        @pl.when(l_up)
        def _():
            result_copy(s).wait_recv()
            returned = (lax.div(owner_ref[s], 2) < chip) & (lane_group >= 2 * GROUP)
            packed[0, s] = jnp.where(returned, ret_r[s], packed[0, s])

        return carry

    lax.fori_loop(0, tiles, settle, 0)
    for k in range(scenes):
        planes = jnp.transpose(packed[k].reshape(tiles * looks, LANES))
        planes = [planes[i * GROUP : (i + 1) * GROUP] for i in range(5)]
        pair_ref[k, 0], pair_ref[k, 1], seq_ref[k, 0], seq_ref[k, 1], coh_ref[k] = planes

    def finish(s, carry):
        candidate_copy(s).wait_send()

        @pl.when(is_l)
        def _():
            handoff_copy(s).wait_send()

        @pl.when(has_outer)
        def _():
            line_copy(s).wait_send()
            relay_copy(s).wait_send()

        @pl.when(r_up)
        def _():
            result_copy(s).wait_send()

        @pl.when(has_left)
        def _():
            edge_copy(s, 0).wait_send()

        @pl.when(has_right)
        def _():
            edge_copy(s, 1).wait_send()

        return carry

    lax.fori_loop(0, tiles, finish, 0)


def local(n_scene, n_range, *operands):
    secondary, store, owner, az_kernel, rg_kernel = operands[:5]
    operands = operands[:3] + (az_kernel.T, rg_kernel.T) + operands[5:]
    scenes, length, _, cols = secondary.shape
    _, tiles, rows = store.shape[:3]
    count, taps = az_kernel.shape
    margin = (length - tiles * rows) // 2
    looks, cells = rows // LOOK_AZ, cols // LOOK_RG
    deep = LOOK_AZ * GROUP
    both = 2 * rows
    image = (both, cols)
    strip = tiles * looks
    dma = pltpu.SemaphoreType.DMA
    vmem = pltpu.VMEM
    home = pl.BlockSpec(memory_space=vmem)
    hbm = pl.BlockSpec(memory_space=pl.ANY)
    dims = (scenes, tiles, rows, cols, margin, taps, n_scene, n_range)
    pairs, sequential, coherent = pl.pallas_call(
        functools.partial(kernel_body, dims),
        out_shape=(
            jax.ShapeDtypeStruct((scenes, 2, cells, strip), F32),
            jax.ShapeDtypeStruct((scenes, 2, cells, strip), F32),
            jax.ShapeDtypeStruct((scenes, cells, strip), F32),
        ),
        in_specs=[hbm] * len(operands),
        out_specs=(home, home, home),
        scratch_shapes=[
            pltpu.SMEM(owner.shape, jnp.int32),
            vmem((taps, count), F32),
            vmem((taps, count), F32),
            vmem((scenes, tiles * rows), jnp.int32),
            vmem((scenes, tiles * rows), jnp.int32),
            vmem((scenes, cols), jnp.int32),
            vmem((scenes, cols), jnp.int32),
            vmem((scenes, 2 * (tiles * rows - deep + LANES), cols), BF16),
            vmem((tiles,) + image, BF16),
            vmem((tiles,) + image, BF16),
            vmem((tiles,) + image, BF16),
            vmem((tiles, scenes) + image, BF16),
            vmem((tiles, scenes) + image, BF16),
            vmem((scenes, rows // deep, 2 * deep, 2 * LANES), BF16),
            vmem((scenes, cols, cols), BF16),
            vmem((scenes, 2 * margin, cols), BF16),
            vmem((count + GROUP, 2 * LANES), BF16),
            vmem((tiles, 2, scenes, margin, both), BF16),
            vmem((tiles, 2, scenes, margin, both), BF16),
            vmem((2, tiles) + image, BF16),
            vmem((tiles,) + image, BF16),
            vmem((tiles,) + image, BF16),
            vmem(image, BF16),
            vmem((tiles, scenes + 2 * (scenes - 1), looks, LANES), F32),
            vmem((scenes, tiles, looks, LANES), F32),
            vmem((tiles, looks, LANES), F32),
            vmem((tiles, looks, LANES), F32),
            dma((7,)),
            dma((scenes,)),
            dma((tiles,)),
            dma((tiles, 2)),
            dma((tiles, 2)),
        ]
        + [dma((tiles,))] * 10,
        compiler_params=pltpu.CompilerParams(
            collective_id=0, has_side_effects=True, vmem_limit_bytes=VMEM_BYTES
        ),
    )(*operands)
    return tuple(jnp.swapaxes(value, -1, -2) for value in (pairs, sequential, coherent))


def solution(mesh):
    in_specs = (
        P(("parts", "scene"), None, None, "range"),
        P(("parts", "scene"), None, None, None, "range"),
        P("parts"),
        P(),
        P(),
        P(("parts", "scene"), None),
        P(("parts", "scene"), None),
        P(("parts", "scene"), "range"),
        P(("parts", "scene"), "range"),
    )
    out_specs = (
        P(("parts", "scene"), None, None, "range"),
        P(("parts", "scene"), None, None, "range"),
        P(("parts", "scene"), None, "range"),
    )
    body = functools.partial(local, mesh.shape["scene"], mesh.shape["range"])
    return jax.shard_map(body, mesh=mesh, in_specs=in_specs, out_specs=out_specs, check_vma=False)
```

time: 47.5 us -> 32.2 us (0.68)
  Pallas kernels: 36.3 us -> 27 us
  local copies, waits for them, and re-layouts: 10.1 us -> 4.32 us
    pallas_call x1, Pallas kernels: 36.3 us -> 27 us  [local(): pl.pallas_call(functools.partial(kernel_body, dims), out_shape=(jax.Shape...]
    unnamed x16 -> x3, local copies, waits for them, and re-layouts: 7.78 us -> 4.32 us
    pallas_call x3 -> x0, local copies, waits for them, and re-layouts: 2.32 us -> none  [local(): pl.pallas_call(functools.partial(kernel_body, (scenes, tiles, rows, cols,...]
where the time goes in v1:
time: 32.2 us; the launch traced here: 32 us
  Pallas kernels  27 us (84%)
  local copies, waits for them, and re-layouts  4.32 us (13%)
  between operations  0.64 us (2%)
    pallas_call x1, Pallas kernels, local(): pl.pallas_call(functools.partial(kernel_body, dims), out_shape=(jax.Shape...  27 us
    unnamed x3, local copies, waits for them, and re-layouts  4.32 us

profile of v1, /device:TPU:0, one launch (start us, length us, event | category | flops | bytes accessed | tf_op | source)
XLA Modules:
  0.0 32.0 jit_solution(12443670625851727474)
XLA Ops:
  0.6 27.0 %shard_map.112 = (f32[2,2,16,256]{3,2,1,0:T(8,128)}, f32[2,2,16,256]{3,2,1,0:T(8,128)}, f32[2,16,256]{2,1,0:T(8,128)}) custom-call(bf16[2,1056,2,256]{3,2,1,0:T(2,128)(2,1)} %sec_hbm.1, bf16[1,4,256,2,256]{4,3,2,1,0:T(2,128)(2,1)} %store_hbm.1, s32[4]{0:T(128)} %owner_hbm.1, f32[8,64]{1,0:T(8,128)} %bitcast.8, f32[8,64]{1,0:T(8,128)} %bitcast.9, ...), custom_call_target="tpu_custom_call" | custom-call | tf_op jit(solution)/shard_map/pallas_call | solution.py:481
  27.6 1.5 %copy.15 = f32[2,2,256,16]{2,3,1,0:T(8,128)} copy(f32[2,2,256,16]{2,3,1,0:T(8,128)} %bitcast.6) | data formatting | bytes 131072
  29.1 1.5 %copy.16 = f32[2,2,256,16]{2,3,1,0:T(8,128)} copy(f32[2,2,256,16]{2,3,1,0:T(8,128)} %bitcast.5) | data formatting | bytes 131072
  30.6 1.4 %copy.17 = f32[2,256,16]{1,2,0:T(8,128)} copy(f32[2,256,16]{1,2,0:T(8,128)} %bitcast.7) | data formatting | bytes 65536

commit v2 on v1

--- a/solution.py
+++ b/solution.py
@@ -11,7 +11,7 @@
 LOOK_RG = 16
 LANES = 128
 GROUP = 16
-VMEM_BYTES = 62 << 20
+VMEM_BYTES = 32 << 20
 
 eps_power = 1e-06
 F32 = jnp.float32
@@ -113,8 +113,8 @@
         pltpu.make_async_copy(source, target, small_sem.at[i])
         for i, (source, target) in enumerate(
             (
-                (rgk_hbm, rgk), (rgo_hbm, rgo), (rgi_hbm, rgi), (azk_hbm, azk),
-                (azo_hbm, azo), (azi_hbm, azi), (owner_hbm, owner_ref),
+                (azk_hbm, azk), (azo_hbm, azo), (azi_hbm, azi), (rgk_hbm, rgk),
+                (rgo_hbm, rgo), (rgi_hbm, rgi), (owner_hbm, owner_ref),
             )
         )
     ]
@@ -123,15 +123,19 @@
         source = store_hbm.reshape(tiles, both, cols).at[s]
         return pltpu.make_async_copy(source, store.at[s], store_sem.at[s])
 
-    def load_sec(k):
-        source = sec_hbm.reshape(scenes, lines, cols).at[k]
-        return pltpu.make_async_copy(source, sec.at[k, pl.ds(0, lines)], sec_sem.at[k])
+    def load_sec(k, s):
+        first, end = (
+            0 if t < 0 else min(lines, (t + 1) * both - 2 * deep + 2 * LANES) for t in (s - 1, s)
+        )
+        length = end - first
+        source = sec_hbm.at[k, pl.ds(first // 2, length // 2)].reshape(length, cols)
+        return pltpu.make_async_copy(source, sec.at[k, pl.ds(first, length)], sec_sem.at[k, s])
 
     for copy in smalls:
         copy.start()
-    for k in range(scenes):
-        load_sec(k).start()
     for s in range(tiles):
+        for k in range(scenes):
+            load_sec(k, s).start()
         load_store(s).start()
 
     barrier = pltpu.get_barrier_semaphore()
@@ -189,22 +193,6 @@
         sec[k, lines:, :] = jnp.zeros((sec.shape[1] - lines, cols), BF16)
 
     for copy in smalls[:3]:
-        copy.wait()
-    rg_table = tap_table(rgk[...], 1)
-    for k in range(scenes):
-        found = looked_up(rg_table, rgi[k : k + 1, :], rgo[k : k + 1, :])
-        tap_rows, shift = found[:, :LANES], found[:, LANES:].astype(jnp.int32)
-        lane = iota((cols, LANES), 1)
-        start = iota((cols, LANES), 0) + shift + (margin - 3)
-        for t in range(cols // LANES):
-            rg_mat[k, :, t * LANES : (t + 1) * LANES] = banded(
-                tap_rows, lane + (t * LANES + margin) - start, taps
-            )
-        beside = jnp.where(lane < margin, lane, lane + cols)
-        beside = jnp.where(lane < 2 * margin, beside, 4 * cols)
-        outside = banded(tap_rows, beside - start, taps).astype(F32)
-        rg_halo[k] = jnp.transpose(outside)[: 2 * margin].astype(BF16)
-    for copy in smalls[3:]:
         copy.wait()
     table[...] = tap_table(azk[...], 2)
 
@@ -240,6 +228,7 @@
             edge[s, 0, k] = ends[:margin]
             edge[s, 1, k] = ends[margin:]
 
+    def send_edges(s):
         @pl.when(has_left)
         def _():
             edge_copy(s, 0).start()
@@ -271,40 +260,6 @@
             value = jnp.where(beyond, relayed[s], value)
         y_send[s] = jnp.where(owner_chip == chip, own[s], value)
         line_copy(s).start()
-
-    pl.semaphore_wait(barrier, sum(exists.astype(jnp.int32) for exists, _ in sides))
-    for s in range(tiles):
-        load_store(s).wait()
-        candidate_copy(s).start()
-    for k in range(scenes):
-        load_sec(k).wait()
-    azimuth(0)
-
-    def resample(s, carry):
-        @pl.when(s + 1 < tiles)
-        def _():
-            azimuth(s + 1)
-
-        range_step(s)
-
-        @pl.when(is_l)
-        def _():
-            handoff_copy(s).start()
-
-        candidate_copy(s).wait_recv()
-        order = by_look(2)
-        for j in range(blocks):
-            at = slice(j * 2 * deep, (j + 1) * 2 * deep)
-            chosen = jnp.where(owner_ref[s] == sibling, other[s, at, :], store[s, at, :])
-            own[s, at, :] = matmul(order, chosen).astype(BF16)
-
-        @pl.when(has_outer & jnp.logical_not(inner))
-        def _():
-            line_send(s, False)
-
-        return carry
-
-    lax.fori_loop(0, tiles, resample, 0)
 
     lane = iota((cols, LANES), 1) & (GROUP - 1)
     start = LOOK_RG * lane
@@ -337,7 +292,7 @@
             out = jnp.where(lane_group < (i + 1) * GROUP, values[i], out)
         return out
 
-    def own_terms(s, carry):
+    def own_terms(s):
         def terms(j, l):
             images = [parts(lambda at, k=k: cur[s, k, at, :], j, l) for k in range(scenes)]
             out = [power(image) for image in images]
@@ -348,9 +303,64 @@
         found = multilooked(scenes + 2 * (scenes - 1), terms)
         for i, value in enumerate(found):
             stats[s, i] = value
+
+    for k in range(scenes):
+        load_sec(k, 0).wait()
+    azimuth(0)
+    pl.semaphore_wait(barrier, sum(exists.astype(jnp.int32) for exists, _ in sides))
+    send_edges(0)
+    for s in range(tiles):
+        load_store(s).wait()
+        candidate_copy(s).start()
+
+    for copy in smalls[3:]:
+        copy.wait()
+    rg_table = tap_table(rgk[...], 1)
+    for k in range(scenes):
+        found = looked_up(rg_table, rgi[k : k + 1, :], rgo[k : k + 1, :])
+        tap_rows, shift = found[:, :LANES], found[:, LANES:].astype(jnp.int32)
+        lane = iota((cols, LANES), 1)
+        start = iota((cols, LANES), 0) + shift + (margin - 3)
+        for t in range(cols // LANES):
+            rg_mat[k, :, t * LANES : (t + 1) * LANES] = banded(
+                tap_rows, lane + (t * LANES + margin) - start, taps
+            )
+        beside = jnp.where(lane < margin, lane, lane + cols)
+        beside = jnp.where(lane < 2 * margin, beside, 4 * cols)
+        outside = banded(tap_rows, beside - start, taps).astype(F32)
+        rg_halo[k] = jnp.transpose(outside)[: 2 * margin].astype(BF16)
+
+    def resample(s, more):
+        candidate_copy(s).wait_recv()
+        order = by_look(2)
+        for j in range(blocks):
+            at = slice(j * 2 * deep, (j + 1) * 2 * deep)
+            chosen = jnp.where(owner_ref[s] == sibling, other[s, at, :], store[s, at, :])
+            own[s, at, :] = matmul(order, chosen).astype(BF16)
+        range_step(s)
+
+        @pl.when(has_outer & jnp.logical_not(inner))
+        def _():
+            line_send(s, False)
+
+        @pl.when(is_l)
+        def _():
+            handoff_copy(s).start()
+
+        if more:
+            azimuth(s + 1)
+            send_edges(s + 1)
+        own_terms(s)
+
+    def resample_step(s, carry):
+        resample(s, True)
         return carry
 
-    lax.fori_loop(0, tiles, own_terms, 0)
+    for s in range(1, tiles):
+        for k in range(scenes):
+            load_sec(k, s).wait()
+    lax.fori_loop(0, tiles - 1, resample_step, 0)
+    resample(tiles - 1, False)
 
     def compare(s, carry):
         def arrived():
@@ -461,9 +471,21 @@
     lax.fori_loop(0, tiles, finish, 0)
 
 
+def write_out(*refs):
+    count = len(refs) // 2
+    copies = [
+        pltpu.make_async_copy(refs[i], refs[count + i], refs[-1].at[i]) for i in range(count)
+    ]
+    for copy in copies:
+        copy.start()
+    for copy in copies:
+        copy.wait()
+
+
 def local(n_scene, n_range, *operands):
     secondary, store, owner, az_kernel, rg_kernel = operands[:5]
     operands = operands[:3] + (az_kernel.T, rg_kernel.T) + operands[5:]
+    operands = [pltpu.with_memory_space_constraint(value, pltpu.HBM) for value in operands]
     scenes, length, _, cols = secondary.shape
     _, tiles, rows = store.shape[:3]
     count, taps = az_kernel.shape
@@ -476,9 +498,9 @@
     dma = pltpu.SemaphoreType.DMA
     vmem = pltpu.VMEM
     home = pl.BlockSpec(memory_space=vmem)
-    hbm = pl.BlockSpec(memory_space=pl.ANY)
+    hbm = pl.BlockSpec(memory_space=pltpu.HBM)
     dims = (scenes, tiles, rows, cols, margin, taps, n_scene, n_range)
-    pairs, sequential, coherent = pl.pallas_call(
+    results = pl.pallas_call(
         functools.partial(kernel_body, dims),
         out_shape=(
             jax.ShapeDtypeStruct((scenes, 2, cells, strip), F32),
@@ -516,7 +538,7 @@
             vmem((tiles, looks, LANES), F32),
             vmem((tiles, looks, LANES), F32),
             dma((7,)),
-            dma((scenes,)),
+            dma((scenes, tiles)),
             dma((tiles,)),
             dma((tiles, 2)),
             dma((tiles, 2)),
@@ -526,7 +548,14 @@
             collective_id=0, has_side_effects=True, vmem_limit_bytes=VMEM_BYTES
         ),
     )(*operands)
-    return tuple(jnp.swapaxes(value, -1, -2) for value in (pairs, sequential, coherent))
+    results = pl.pallas_call(
+        write_out,
+        out_shape=[jax.ShapeDtypeStruct(value.shape, F32) for value in results],
+        in_specs=[home] * len(results),
+        out_specs=[hbm] * len(results),
+        scratch_shapes=[dma((len(results),))],
+    )(*results)
+    return tuple(jnp.swapaxes(value, -1, -2) for value in results)
 
 
 def solution(mesh):

time: 32.2 us -> 36.9 us (1.15)
  Pallas kernels: 27 us -> 34.2 us
  local copies, waits for them, and re-layouts: 4.32 us -> 1.85 us
    pallas_call x1, Pallas kernels: 27 us -> 32.7 us  [local(): pl.pallas_call(functools.partial(kernel_body, dims), out_shape=(jax.Shape...]
    unnamed x3 -> x6, local copies, waits for them, and re-layouts: 4.32 us -> 1.85 us
    pallas_call x0 -> x1, Pallas kernels: none -> 1.55 us  [local(): pl.pallas_call(write_out, out_shape=[jax.ShapeDtypeStruct(value.shape, F3...]
where the time goes in v2:
time: 36.9 us; the launch traced here: 36.8 us
  Pallas kernels  34.2 us (93%)
  local copies, waits for them, and re-layouts  1.85 us (5%)
  between operations  0.65 us (2%)
    pallas_call x1, Pallas kernels, local(): pl.pallas_call(functools.partial(kernel_body, dims), out_shape=(jax.Shape...  32.7 us
    unnamed x6, local copies, waits for them, and re-layouts  1.85 us
    pallas_call x1, Pallas kernels, local(): pl.pallas_call(write_out, out_shape=[jax.ShapeDtypeStruct(value.shape, F3...  1.55 us

profile of v2, /device:TPU:0, one launch (start us, length us, event | category | flops | bytes accessed | tf_op | source)
XLA Modules:
  0.0 36.8 jit_solution(7325203872384995343)
XLA Ops:
  0.6 32.7 %shard_map.112 = (f32[2,2,16,256]{3,2,1,0:T(8,128)S(1)}, f32[2,2,16,256]{3,2,1,0:T(8,128)S(1)}, f32[2,16,256]{2,1,0:T(8,128)S(1)}) custom-call(bf16[2,1056,2,256]{3,2,1,0:T(2,128)(2,1)} %sec_hbm.1, bf16[1,4,256,2,256]{4,3,2,1,0:T(2,128)(2,1)} %store_hbm.1, s32[4]{0:T(128)} %owner_hbm.1, f32[8,64]{1,0:T(8,128)} %bitcast.5, f32[8,64]{1,0:T(8,128)} %bitcast.6, ...), custom_call_target="tpu_custom_call" | custom-call | tf_op jit(solution)/shard_map/pallas_call | solution.py:503
  33.3 0.0 copy-start
  33.3 0.6 %copy-done = f32[2,2,16,256]{3,2,1,0:T(8,128)} copy-done((f32[2,2,16,256]{3,2,1,0:T(8,128)}, f32[2,2,16,256]{3,2,1,0:T(8,128)S(1)}, u32[]{:S(2)}) %copy-start) | copy-done | bytes 65560
  34.0 0.0 copy-start.1
  34.0 0.6 %copy-done.1 = f32[2,2,16,256]{3,2,1,0:T(8,128)} copy-done((f32[2,2,16,256]{3,2,1,0:T(8,128)}, f32[2,2,16,256]{3,2,1,0:T(8,128)S(1)}, u32[]{:S(2)}) %copy-start.1) | copy-done | bytes 65560
  34.6 0.0 copy-start.2
  34.6 0.6 %copy-done.2 = f32[2,16,256]{2,1,0:T(8,128)} copy-done((f32[2,16,256]{2,1,0:T(8,128)}, f32[2,16,256]{2,1,0:T(8,128)S(1)}, u32[]{:S(2)}) %copy-start.2) | copy-done | bytes 32792
  35.2 1.6 %shard_map.113 = (f32[2,2,16,256]{3,2,1,0:T(8,128)}, f32[2,2,16,256]{3,2,1,0:T(8,128)}, f32[2,16,256]{2,1,0:T(8,128)}) custom-call(f32[2,2,16,256]{3,2,1,0:T(8,128)} %copy-done, f32[2,2,16,256]{3,2,1,0:T(8,128)} %copy-done.1, f32[2,16,256]{2,1,0:T(8,128)} %copy-done.2), custom_call_target="tpu_custom_call" | custom-call | tf_op jit(solution)/shard_map/pallas_call | solution.py:551
Async XLA Ops:
  33.3 0.6 %copy-start = (f32[2,2,16,256]{3,2,1,0:T(8,128)}, f32[2,2,16,256]{3,2,1,0:T(8,128)S(1)}, u32[]{:S(2)}) copy-start(f32[2,2,16,256]{3,2,1,0:T(8,128)S(1)} %get-tuple-element.9.refs_0_) | copy-start | bytes 196612
  34.0 0.6 %copy-start.1 = (f32[2,2,16,256]{3,2,1,0:T(8,128)}, f32[2,2,16,256]{3,2,1,0:T(8,128)S(1)}, u32[]{:S(2)}) copy-start(f32[2,2,16,256]{3,2,1,0:T(8,128)S(1)} %get-tuple-element.10.refs_1_) | copy-start | bytes 196612
  34.6 0.6 %copy-start.2 = (f32[2,16,256]{2,1,0:T(8,128)}, f32[2,16,256]{2,1,0:T(8,128)S(1)}, u32[]{:S(2)}) copy-start(f32[2,16,256]{2,1,0:T(8,128)S(1)} %get-tuple-element.11.refs_2_) | copy-start | bytes 98308

commit v3 on v2

--- a/solution.py
+++ b/solution.py
@@ -11,6 +11,7 @@
 LOOK_RG = 16
 LANES = 128
 GROUP = 16
+EARLY = 2
 VMEM_BYTES = 32 << 20
 
 eps_power = 1e-06
@@ -134,8 +135,11 @@
     for copy in smalls:
         copy.start()
     for s in range(tiles):
+        if s < EARLY:
+            load_store(s).start()
         for k in range(scenes):
             load_sec(k, s).start()
+    for s in range(EARLY, tiles):
         load_store(s).start()
 
     barrier = pltpu.get_barrier_semaphore()
@@ -178,12 +182,15 @@
         source = cur.at[s, scenes - 1]
         return remote(source, comm.at[0, s], hs_sem.at[s], hr_sem.at[s], {"scene": sibling})
 
-    def line_copy(s):
-        target = comm.at[1 - core, s]
-        return remote(y_send.at[s], target, ys_sem.at[s], yr_sem.at[s], {"scene": outer})
+    def ref_message(s):
+        return jnp.where(s < EARLY, s + tiles, s)
+
+    def line_copy(m):
+        target = comm.at[1 - core, m]
+        return remote(y_send.at[m], target, ys_sem.at[m], yr_sem.at[m], {"scene": outer})
 
     def relay_copy(s):
-        source = comm.at[core, s]
+        source = comm.at[core, ref_message(s)]
         return remote(source, relayed.at[s], ls_sem.at[s], lr_sem.at[s], {"scene": sibling})
 
     def result_copy(s):
@@ -248,7 +255,7 @@
 
         for k in range(scenes):
             beside = jnp.concatenate([halo[s, 0, k], halo[s, 1, k]], 0)
-            total = matmul(z[s, k], rg_mat[k], ((1,), (1,)))
+            total = matmul(z[s, k], rg_mat[k])
             total = total + matmul(beside, rg_halo[k], ((0,), (0,)))
             cur[s, k] = total.astype(BF16)
 
@@ -258,8 +265,25 @@
         if from_relay:
             beyond = (is_r & (owner_chip < chip)) | (is_l & (owner_chip > chip))
             value = jnp.where(beyond, relayed[s], value)
-        y_send[s] = jnp.where(owner_chip == chip, own[s], value)
-        line_copy(s).start()
+        m = ref_message(s)
+        y_send[m] = jnp.where(owner_chip == chip, own[s], value)
+        line_copy(m).start()
+
+    def choose(s):
+        candidate_copy(s).wait_recv()
+        order = by_look(2)
+        for j in range(blocks):
+            at = slice(j * 2 * deep, (j + 1) * 2 * deep)
+            chosen = jnp.where(owner_ref[s] == sibling, other[s, at, :], store[s, at, :])
+            own[s, at, :] = matmul(order, chosen).astype(BF16)
+
+    def hands_on(s):
+        even = lax.rem(s, 2) == 0
+        return (s < EARLY) & ((r_up & even) | (l_up & jnp.logical_not(even)))
+
+    def gets_handed(s):
+        even = lax.rem(s, 2) == 0
+        return (s < EARLY) & ((l_up & even) | (r_up & jnp.logical_not(even)))
 
     lane = iota((cols, LANES), 1) & (GROUP - 1)
     start = LOOK_RG * lane
@@ -304,16 +328,28 @@
         for i, value in enumerate(found):
             stats[s, i] = value
 
+    pl.semaphore_wait(barrier, sum(exists.astype(jnp.int32) for exists, _ in sides))
+    for s in range(EARLY):
+        load_store(s).wait()
+        candidate_copy(s).start()
     for k in range(scenes):
         load_sec(k, 0).wait()
     azimuth(0)
-    pl.semaphore_wait(barrier, sum(exists.astype(jnp.int32) for exists, _ in sides))
     send_edges(0)
-    for s in range(tiles):
+    smalls[-1].wait()
+    for s in range(EARLY):
+        choose(s)
+
+        @pl.when(has_outer & jnp.logical_not(inner))
+        def _():
+            y_send[tiles + s] = own[s]
+            line_copy(tiles + s).start()
+
+    for s in range(EARLY, tiles):
         load_store(s).wait()
         candidate_copy(s).start()
 
-    for copy in smalls[3:]:
+    for copy in smalls[3:-1]:
         copy.wait()
     rg_table = tap_table(rgk[...], 1)
     for k in range(scenes):
@@ -322,34 +358,36 @@
         lane = iota((cols, LANES), 1)
         start = iota((cols, LANES), 0) + shift + (margin - 3)
         for t in range(cols // LANES):
-            rg_mat[k, :, t * LANES : (t + 1) * LANES] = banded(
-                tap_rows, lane + (t * LANES + margin) - start, taps
-            )
+            found = banded(tap_rows, lane + (t * LANES + margin) - start, taps).astype(F32)
+            rg_mat[k, t * LANES : (t + 1) * LANES, :] = jnp.transpose(found).astype(BF16)
         beside = jnp.where(lane < margin, lane, lane + cols)
         beside = jnp.where(lane < 2 * margin, beside, 4 * cols)
         outside = banded(tap_rows, beside - start, taps).astype(F32)
         rg_halo[k] = jnp.transpose(outside)[: 2 * margin].astype(BF16)
 
     def resample(s, more):
-        candidate_copy(s).wait_recv()
-        order = by_look(2)
-        for j in range(blocks):
-            at = slice(j * 2 * deep, (j + 1) * 2 * deep)
-            chosen = jnp.where(owner_ref[s] == sibling, other[s, at, :], store[s, at, :])
-            own[s, at, :] = matmul(order, chosen).astype(BF16)
-        range_step(s)
-
-        @pl.when(has_outer & jnp.logical_not(inner))
-        def _():
-            line_send(s, False)
-
-        @pl.when(is_l)
-        def _():
-            handoff_copy(s).start()
-
         if more:
             azimuth(s + 1)
             send_edges(s + 1)
+        range_step(s)
+
+        @pl.when(hands_on(s))
+        def _():
+            y_send[s] = cur[s, core * (scenes - 1)]
+            line_copy(s).start()
+
+        @pl.when(s >= EARLY)
+        def _():
+            choose(s)
+
+            @pl.when(has_outer & jnp.logical_not(inner))
+            def _():
+                line_send(s, False)
+
+        @pl.when(is_l)
+        def _():
+            handoff_copy(s).start()
+
         own_terms(s)
 
     def resample_step(s, carry):
@@ -364,7 +402,7 @@
 
     def compare(s, carry):
         def arrived():
-            line_copy(s).wait_recv()
+            line_copy(ref_message(s)).wait_recv()
             relay_copy(s).start()
 
         def handed():
@@ -379,6 +417,10 @@
         pl.when(r_up)(arrived)
         pl.when(is_l & has_next)(handed)
 
+        @pl.when(gets_handed(s))
+        def _():
+            line_copy(s).wait_recv()
+
         @pl.when(is_r)
         def _():
             handoff_copy(s).wait_recv()
@@ -397,7 +439,7 @@
 
         owner_chip = lax.div(owner_ref[s], 2)
         direct = (is_l & (owner_chip < chip)) | (is_r & (owner_chip > chip))
-        far = jnp.where(direct, comm[core, s], relayed[s])
+        far = jnp.where(direct, comm[core, ref_message(s)], relayed[s])
         ref[...] = jnp.where(owner_chip == chip, own[s], far)
 
         @pl.when(me == 0)
@@ -431,7 +473,9 @@
         @pl.when(l_up)
         def _():
             result_copy(s).wait_recv()
-            returned = (lax.div(owner_ref[s], 2) < chip) & (lane_group >= 2 * GROUP)
+            owner_chip = lax.div(owner_ref[s], 2)
+            back = ((s < EARLY) & (lax.rem(s, 2) == 1)) | ((s >= EARLY) & (owner_chip < chip))
+            returned = back & (lane_group >= 2 * GROUP)
             packed[0, s] = jnp.where(returned, ret_r[s], packed[0, s])
 
         return carry
@@ -451,8 +495,12 @@
 
         @pl.when(has_outer)
         def _():
+            line_copy(ref_message(s)).wait_send()
+            relay_copy(s).wait_send()
+
+        @pl.when(hands_on(s))
+        def _():
             line_copy(s).wait_send()
-            relay_copy(s).wait_send()
 
         @pl.when(r_up)
         def _():
@@ -529,9 +577,9 @@
             vmem((count + GROUP, 2 * LANES), BF16),
             vmem((tiles, 2, scenes, margin, both), BF16),
             vmem((tiles, 2, scenes, margin, both), BF16),
-            vmem((2, tiles) + image, BF16),
+            vmem((2, tiles + EARLY) + image, BF16),
             vmem((tiles,) + image, BF16),
-            vmem((tiles,) + image, BF16),
+            vmem((tiles + EARLY,) + image, BF16),
             vmem(image, BF16),
             vmem((tiles, scenes + 2 * (scenes - 1), looks, LANES), F32),
             vmem((scenes, tiles, looks, LANES), F32),
@@ -543,7 +591,9 @@
             dma((tiles, 2)),
             dma((tiles, 2)),
         ]
-        + [dma((tiles,))] * 10,
+        + [dma((tiles,))] * 4
+        + [dma((tiles + EARLY,))] * 2
+        + [dma((tiles,))] * 4,
         compiler_params=pltpu.CompilerParams(
             collective_id=0, has_side_effects=True, vmem_limit_bytes=VMEM_BYTES
         ),
@@ -551,10 +601,10 @@
     results = pl.pallas_call(
         write_out,
         out_shape=[jax.ShapeDtypeStruct(value.shape, F32) for value in results],
-        in_specs=[home] * len(results),
+        in_specs=[hbm] * len(results),
         out_specs=[hbm] * len(results),
         scratch_shapes=[dma((len(results),))],
-    )(*results)
+    )(*[pltpu.with_memory_space_constraint(value, pltpu.HBM) for value in results])
     return tuple(jnp.swapaxes(value, -1, -2) for value in results)
 
 

time: 36.9 us -> 35.6 us (0.965)
  Pallas kernels: 34.2 us -> 32.9 us
    pallas_call x1, Pallas kernels: 32.7 us -> 26.8 us  [local(): pl.pallas_call(functools.partial(kernel_body, dims), out_shape=(jax.Shape...]
    pallas_call x1, Pallas kernels: 1.55 us -> 6.09 us  [local(): pl.pallas_call(write_out, out_shape=[jax.ShapeDtypeStruct(value.shape, F3...]
where the time goes in v3:
time: 35.6 us; the launch traced here: 35.4 us
  Pallas kernels  32.9 us (92%)
  local copies, waits for them, and re-layouts  1.85 us (5%)
  between operations  0.65 us (2%)
    pallas_call x1, Pallas kernels, local(): pl.pallas_call(functools.partial(kernel_body, dims), out_shape=(jax.Shape...  26.8 us
    pallas_call x1, Pallas kernels, local(): pl.pallas_call(write_out, out_shape=[jax.ShapeDtypeStruct(value.shape, F3...  6.09 us
    unnamed x6, local copies, waits for them, and re-layouts  1.85 us

profile of v3, /device:TPU:0, one launch (start us, length us, event | category | flops | bytes accessed | tf_op | source)
XLA Modules:
  0.0 35.4 jit_solution(14554595110166365392)
XLA Ops:
  0.6 26.8 %shard_map.112 = (f32[2,2,16,256]{3,2,1,0:T(8,128)S(1)}, f32[2,2,16,256]{3,2,1,0:T(8,128)S(1)}, f32[2,16,256]{2,1,0:T(8,128)S(1)}) custom-call(bf16[2,1056,2,256]{3,2,1,0:T(2,128)(2,1)} %sec_hbm.1, bf16[1,4,256,2,256]{4,3,2,1,0:T(2,128)(2,1)} %store_hbm.1, s32[4]{0:T(128)} %owner_hbm.1, f32[8,64]{1,0:T(8,128)} %bitcast.5, f32[8,64]{1,0:T(8,128)} %bitcast.6, ...), custom_call_target="tpu_custom_call" | custom-call | tf_op jit(solution)/shard_map/pallas_call | solution.py:551
  27.5 0.0 copy-start
  27.5 0.6 %copy-done = f32[2,2,16,256]{3,2,1,0:T(8,128)} copy-done((f32[2,2,16,256]{3,2,1,0:T(8,128)}, f32[2,2,16,256]{3,2,1,0:T(8,128)S(1)}, u32[]{:S(2)}) %copy-start) | copy-done | bytes 65560
  28.1 0.0 copy-start.1
  28.1 0.6 %copy-done.1 = f32[2,2,16,256]{3,2,1,0:T(8,128)} copy-done((f32[2,2,16,256]{3,2,1,0:T(8,128)}, f32[2,2,16,256]{3,2,1,0:T(8,128)S(1)}, u32[]{:S(2)}) %copy-start.1) | copy-done | bytes 65560
  28.7 0.0 copy-start.2
  28.7 0.6 %copy-done.2 = f32[2,16,256]{2,1,0:T(8,128)} copy-done((f32[2,16,256]{2,1,0:T(8,128)}, f32[2,16,256]{2,1,0:T(8,128)S(1)}, u32[]{:S(2)}) %copy-start.2) | copy-done | bytes 32792
  29.3 6.1 %shard_map.113 = (f32[2,2,16,256]{3,2,1,0:T(8,128)}, f32[2,2,16,256]{3,2,1,0:T(8,128)}, f32[2,16,256]{2,1,0:T(8,128)}) custom-call(f32[2,2,16,256]{3,2,1,0:T(8,128)} %copy-done, f32[2,2,16,256]{3,2,1,0:T(8,128)} %copy-done.1, f32[2,16,256]{2,1,0:T(8,128)} %copy-done.2), custom_call_target="tpu_custom_call" | custom-call | tf_op jit(solution)/shard_map/pallas_call | solution.py:601
Async XLA Ops:
  27.5 0.6 %copy-start = (f32[2,2,16,256]{3,2,1,0:T(8,128)}, f32[2,2,16,256]{3,2,1,0:T(8,128)S(1)}, u32[]{:S(2)}) copy-start(f32[2,2,16,256]{3,2,1,0:T(8,128)S(1)} %get-tuple-element.9.refs_0_) | copy-start | bytes 196612
  28.1 0.6 %copy-start.1 = (f32[2,2,16,256]{3,2,1,0:T(8,128)}, f32[2,2,16,256]{3,2,1,0:T(8,128)S(1)}, u32[]{:S(2)}) copy-start(f32[2,2,16,256]{3,2,1,0:T(8,128)S(1)} %get-tuple-element.10.refs_1_) | copy-start | bytes 196612
  28.7 0.6 %copy-start.2 = (f32[2,16,256]{2,1,0:T(8,128)}, f32[2,16,256]{2,1,0:T(8,128)S(1)}, u32[]{:S(2)}) copy-start(f32[2,16,256]{2,1,0:T(8,128)S(1)} %get-tuple-element.11.refs_2_) | copy-start | bytes 98308

commit v4 on v3

--- a/solution.py
+++ b/solution.py
@@ -517,17 +517,6 @@
         return carry
 
     lax.fori_loop(0, tiles, finish, 0)
-
-
-def write_out(*refs):
-    count = len(refs) // 2
-    copies = [
-        pltpu.make_async_copy(refs[i], refs[count + i], refs[-1].at[i]) for i in range(count)
-    ]
-    for copy in copies:
-        copy.start()
-    for copy in copies:
-        copy.wait()
 
 
 def local(n_scene, n_range, *operands):
@@ -598,13 +587,6 @@
             collective_id=0, has_side_effects=True, vmem_limit_bytes=VMEM_BYTES
         ),
     )(*operands)
-    results = pl.pallas_call(
-        write_out,
-        out_shape=[jax.ShapeDtypeStruct(value.shape, F32) for value in results],
-        in_specs=[hbm] * len(results),
-        out_specs=[hbm] * len(results),
-        scratch_shapes=[dma((len(results),))],
-    )(*[pltpu.with_memory_space_constraint(value, pltpu.HBM) for value in results])
     return tuple(jnp.swapaxes(value, -1, -2) for value in results)
 
 

time: 35.6 us -> 29.5 us (0.83)
  Pallas kernels: 32.9 us -> 26.8 us
    pallas_call x1 -> x0, Pallas kernels: 6.09 us -> none  [local(): pl.pallas_call(write_out, out_shape=[jax.ShapeDtypeStruct(value.shape, F3...]
    unnamed x6 -> x3, local copies, waits for them, and re-layouts: 1.85 us -> 1.88 us
where the time goes in v4:
time: 29.5 us; the launch traced here: 29.3 us
  Pallas kernels  26.8 us (91%)
  local copies, waits for them, and re-layouts  1.88 us (6%)
  between operations  0.64 us (2%)
    pallas_call x1, Pallas kernels, local(): pl.pallas_call(functools.partial(kernel_body, dims), out_shape=(jax.Shape...  26.8 us
    unnamed x3, local copies, waits for them, and re-layouts  1.88 us

profile of v4, /device:TPU:0, one launch (start us, length us, event | category | flops | bytes accessed | tf_op | source)
XLA Modules:
  0.0 29.3 jit_solution(15418688096937742513)
XLA Ops:
  0.6 26.8 %shard_map.112 = (f32[2,2,16,256]{3,2,1,0:T(8,128)S(1)}, f32[2,2,16,256]{3,2,1,0:T(8,128)S(1)}, f32[2,16,256]{2,1,0:T(8,128)S(1)}) custom-call(bf16[2,1056,2,256]{3,2,1,0:T(2,128)(2,1)} %sec_hbm.1, bf16[1,4,256,2,256]{4,3,2,1,0:T(2,128)(2,1)} %store_hbm.1, s32[4]{0:T(128)} %owner_hbm.1, f32[8,64]{1,0:T(8,128)} %bitcast.8, f32[8,64]{1,0:T(8,128)} %bitcast.9, ...), custom_call_target="tpu_custom_call" | custom-call | tf_op jit(solution)/shard_map/pallas_call | solution.py:540
  27.5 0.6 %copy.15 = f32[2,2,256,16]{2,3,1,0:T(8,128)} copy(f32[2,2,256,16]{2,3,1,0:T(8,128)S(1)} %bitcast.6) | data formatting | bytes 131072
  28.1 0.6 %copy.16 = f32[2,2,256,16]{2,3,1,0:T(8,128)} copy(f32[2,2,256,16]{2,3,1,0:T(8,128)S(1)} %bitcast.5) | data formatting | bytes 131072
  28.7 0.6 %copy.17 = f32[2,256,16]{1,2,0:T(8,128)} copy(f32[2,256,16]{1,2,0:T(8,128)S(1)} %bitcast.7) | data formatting | bytes 65536
